TPU v7x, 32 devices: a whole 2x2x4 slice. The times are simulated.
32 devices in a mesh: groups: 2 (over x), blk: 8 (over z, y), split: 2 (over core).
Axes of the slice: x: 2, y: 2, z: 4, core: 2. Of those that a mesh axis runs over, the one named last changes fastest.
Arguments:
- tiles: bfloat16 [8192, 1536], P(('groups', 'blk')), parts along dimension 0, may hold values from -6 to 6
- landmarks: bfloat16 [2048, 1536], P(('blk', 'split')), may hold values from -6 to 6
- projection: bfloat16 [2048, 1024], P(('blk', 'split')), may hold values from -0.125 to 0.125
- offsets: float32 [2048], P(('blk', 'split')), may hold values from 0 to 2
Outputs:
- coords: bfloat16 [8192, 1024], P(('groups', 'blk')), parts along dimension 0
- energy: float32 [8192], P(('groups', 'blk')), parts along dimension 0
There are 2 independent parts, one for each index of `groups`. A program takes and returns all parts, laid end to end along the dimension named above; an argument that names none is the same for every part. Nothing has to cross between parts.
All inputs are finite; a program needn't handle non-finite values.
Results may differ from a plain program's by a relative error of at most 0.012.
Values may be sent and summed in bfloat16 or wider, within the bound.
A program may use at most 64 MiB of HBM per device.

v0:
```python
import jax
import jax.numpy as jnp
from jax import lax
from jax.sharding import PartitionSpec as P


def block_term(tiles, land, proj, off):
    scale = 1.0 / tiles.shape[1] ** 0.5
    scores = lax.dot_general(
        tiles, land, (((1,), (1,)), ((), ())), preferred_element_type=jnp.float32
    )
    kernel = jnp.exp(scores * scale - off[None, :]).astype(jnp.bfloat16)
    return jnp.dot(kernel, proj, preferred_element_type=jnp.float32)


def per_device(tiles, landmarks, projection, offsets):
    width_k = projection.shape[1]
    partial_sum = block_term(
        tiles,
        lax.all_gather(landmarks, "blk", axis=0, tiled=True),
        lax.all_gather(projection, "blk", axis=0, tiled=True),
        lax.all_gather(offsets.astype(jnp.bfloat16), "blk", axis=0, tiled=True).astype(jnp.float32),
    )
    share = lax.psum_scatter(
        partial_sum.astype(jnp.bfloat16), "split", scatter_dimension=1, tiled=True
    ).astype(jnp.float32)
    squares = lax.psum(jnp.sum(share * share, axis=1), "split")
    energy = jnp.log(squares / width_k + 1e-06)
    coords = lax.all_gather(share.astype(jnp.bfloat16), "split", axis=1, tiled=True)
    return (coords, energy)


def solution(mesh):
    return jax.shard_map(
        per_device,
        mesh=mesh,
        in_specs=(
            P(("groups", "blk"), None),
            P(("blk", "split"), None),
            P(("blk", "split"), None),
            P(("blk", "split")),
        ),
        out_specs=(P(("groups", "blk"), None), P(("groups", "blk"))),
        check_vma=False,
    )
```

profile of v0, /device:TPU:0, one launch (start us, length us, event | category | flops | bytes accessed | tf_op | source)
XLA Modules:
  0.0 157.7 jit_solution(7599696476700320605)
XLA Ops:
  7.2 0.0 copy-start
  7.2 0.0 all-gather.7.cloned.1.call-start
  7.2 0.7 all-gather.7.cloned.1.call-update
  7.9 0.0 all-gather.5.cloned.1.call-start
  8.0 0.7 all-gather.5.cloned.1.call-update
  8.7 0.0 reduce-scatter.2.cloned.1.call-start
  8.7 0.7 convert_bitcast_fusion
  9.4 22.2 %all-gather = bf16[8,1,128]{2,1,0:T(2,128)(2,1)S(1)} all-gather(bf16[1,1,128]{2,1,0:T(2,128)(2,1)S(1)} %convert_bitcast_fusion), channel_id=1, replica_groups=mesh['groups'=2,'blk'=8,'split'=2] {'blk'}, dimensions={0}, use_global_device_ids=true | all-gather | bytes 2304 | tf_op jit(solution)/shard_map/all_gather | solution.py:22
  31.5 30.6 %all-gather.7.cloned.1.call-done = bf16[1024,1024]{1,0:T(8,128)(2,1)} async-done(((bf16[128,1024]{1,0:T(8,128)(2,1)}), bf16[1024,1024]{1,0:T(8,128)(2,1)}) %all-gather.7.cloned.1.call-update) | async-done | bytes 2097168 | tf_op jit(solution)/shard_map/all_gather | solution.py:21
  62.2 61.2 %all-gather.5.cloned.1.call-done = bf16[1024,1536]{1,0:T(8,128)(2,1)} async-done(((bf16[128,1536]{1,0:T(8,128)(2,1)}), bf16[1024,1536]{1,0:T(8,128)(2,1)}) %all-gather.5.cloned.1.call-update) | async-done | bytes 3145744 | tf_op jit(solution)/shard_map/all_gather | solution.py:20
  123.3 0.0 copy-done
  123.3 6.5 %convolution_convert_fusion = bf16[512,1024]{1,0:T(8,128)(2,1)} fusion(bf16[1024,1024]{1,0:T(8,128)(2,1)} %all-gather.7.cloned.1.call-done, bf16[512,1536]{1,0:T(8,128)(2,1)S(1)} %copy-done, bf16[1024,1536]{1,0:T(8,128)(2,1)} %all-gather.5.cloned.1.call-done, f32[1024]{0:T(1024)S(1)} %bitcast.6), kind=kOutput, calls=%fused_computation.1 | convolution fusion | flops 2686451712 | bytes 7868416 | tf_op jit(solution)/shard_map/dot_general | solution.py:13
  129.8 0.0 reduce-scatter.2.cloned.1.call-update
  129.9 0.0 all-gather.9.cloned.1.call-start
  129.9 7.3 %reduce-scatter.2.cloned.1.call-done = bf16[512,512]{1,0:T(8,128)(2,1)} async-done(((bf16[512,1024]{1,0:T(8,128)(2,1)}), bf16[512,512]{1,0:T(8,128)(2,1)}) %reduce-scatter.2.cloned.1.call-update) | async-done | bytes 524304 | tf_op jit(solution)/shard_map/reduce_scatter | solution.py:24
  137.2 0.0 all-gather.9.cloned.1.call-update
  137.2 1.2 multiply_reduce_fusion
  138.4 2.5 %psum.7 = f32[512]{0:T(512)S(1)} all-reduce(f32[512]{0:T(512)S(1)} %multiply_reduce_fusion), channel_id=1, replica_groups=mesh['groups'=2,'blk'=8,'split'=2] {'split'}, use_global_device_ids=true, to_apply=%region_2.0 | all-reduce | flops 512 | bytes 4096 | tf_op jit(solution)/shard_map/psum | solution.py:27
  140.9 0.6 add_log_fusion
  141.5 7.4 %all-gather.9.cloned.1.call-done = bf16[512,1024]{1,0:T(8,128)(2,1)} async-done(((bf16[512,512]{1,0:T(8,128)(2,1)}), bf16[512,1024]{1,0:T(8,128)(2,1)}) %all-gather.9.cloned.1.call-update) | async-done | bytes 1048592 | tf_op jit(solution)/shard_map/all_gather | solution.py:29
  148.9 2.3 %copy.7 = bf16[512,1024]{1,0:T(8,128)(2,1)} copy(bf16[512,1024]{1,0:T(8,128)(2,1)} %all-gather.9.cloned.1.call-done) | data formatting | bytes 2097152
  (1 shorter events, 0.0 us)
Async XLA Ops:
  7.2 116.2 %copy-start = (bf16[512,1536]{1,0:T(8,128)(2,1)S(1)}, bf16[512,1536]{1,0:T(8,128)(2,1)}, u32[]{:S(2)}) copy-start(bf16[512,1536]{1,0:T(8,128)(2,1)} %param.4) | copy-start | bytes 4718596
  7.2 55.0 %all-gather.7.cloned.1.call-start = ((), (), s32[]{:S(2)}) async-start(), calls=%async_computation.2 | async-start | bytes 2359296 | tf_op jit(solution)/shard_map/all_gather | solution.py:21
  7.9 115.4 %all-gather.5.cloned.1.call-start = ((), (), s32[]{:S(2)}) async-start(), calls=%async_computation.1 | async-start | bytes 3538944 | tf_op jit(solution)/shard_map/all_gather | solution.py:20
  8.7 128.5 %reduce-scatter.2.cloned.1.call-start = ((), (), s32[]{:S(2)}) async-start(), calls=%async_computation.3 | async-start | bytes 1572864 | tf_op jit(solution)/shard_map/reduce_scatter | solution.py:24
  129.9 19.0 %all-gather.9.cloned.1.call-start = ((), (), s32[]{:S(2)}) async-start(), calls=%async_computation.4 | async-start | bytes 1572864 | tf_op jit(solution)/shard_map/all_gather | solution.py:29
Sparse Core Ops, SparseCore 0:
  10.1 51.9 all-gather.6
  64.3 58.9 all-gather.4
  130.0 7.1 reduce-scatter.1
  138.7 10.1 all-gather.8
where the time goes:
time: 158 us
  waiting for transfers between devices  108 us (68%)
  blocking collectives  24.6 us (16%)
  between operations  13.8 us (9%)
  matrix products  6.51 us (4%)
  other arithmetic  2.47 us (2%)
  local copies, waits for them, and re-layouts  2.27 us (1%)
    all_gather x1, waiting for transfers between devices, per_device(): lax.all_gather(landmarks, 'blk', axis=0, tiled=True)  61.2 us
    all_gather x1, waiting for transfers between devices, per_device(): lax.all_gather(projection, 'blk', axis=0, tiled=True)  30.6 us
    all_gather x1, blocking collectives, per_device(): lax.all_gather(offsets.astype(jnp.bfloat16), 'blk', axis=0, tiled=True)  22.2 us
    all_gather x1, waiting for transfers between devices, per_device(): lax.all_gather(share.astype(jnp.bfloat16), 'split', axis=1, tiled=True)  7.41 us
    reduce_scatter x1, waiting for transfers between devices, per_device(): lax.psum_scatter(partial_sum.astype(jnp.bfloat16), 'split', scatter_dimen...  7.27 us
    dot_general x1, matrix products, block_term(): return jnp.dot(kernel, proj, preferred_element_type=jnp.float32)  6.51 us
  transfers between devices with their start and end apart: 4, of which 4 were waited for; matrix products, arithmetic and copies ran while one was open for 2% of the time, Pallas kernels for 0%

commit v1 on v0

v1 whole, which is shorter than its diff:
```python
import functools

import jax
import jax.numpy as jnp
from jax import lax
from jax.experimental import pallas as pl
from jax.experimental.pallas import tpu as pltpu
from jax.sharding import PartitionSpec as P

MESH = pl.DeviceIdType.MESH
UP, DOWN, ACROSS, SIB = 0, 1, 2, 3


def kernel(
    nb, ny, chunks,
    tiles, land, proj, off, out, energy,
    t_buf, l_buf, o_buf, p_buf, k_buf, acc, x_out, x_in, c_buf, e_buf, sq,
    r_land, r_off, r_proj, s_land, s_off, s_proj,
    loc_sem, t_send, t_recv, xs_sem, xr_sem, c_send, c_recv, c_loc, e_sem,
):
    nz = nb // ny
    g, me, s = lax.axis_index("groups"), lax.axis_index("blk"), lax.axis_index("split")
    half = lax.rem(g, 2)
    z, y = me // ny, lax.rem(me, ny)
    rows_t = t_buf.shape[0] // 2
    hr = l_buf.shape[2]
    width_k = acc.shape[1]
    kc = width_k // chunks
    scale = 1.0 / l_buf.shape[3] ** 0.5

    mate = {"groups": g + 1 - 2 * half}
    sib = {"split": 1 - s}
    peers = {
        UP: ({"blk": me + ny}, z + 1 < nz),
        DOWN: ({"blk": me - ny}, z > 0),
        ACROSS: ({"blk": me + 1 - 2 * y}, None),
        SIB: (sib, None),
    }
    dirs = [UP, DOWN, SIB] + ([ACROSS] if ny == 2 else [])

    def guard(cond, fn):
        if cond is None:
            fn()
        else:
            pl.when(cond)(fn)

    barrier = pltpu.get_barrier_semaphore()

    def greet(dev):
        pl.semaphore_signal(barrier, inc=1, device_id=dev, device_id_type=MESH)

    greet(mate)
    for d in dirs:
        guard(peers[d][1], functools.partial(greet, peers[d][0]))
    pl.semaphore_wait(
        barrier,
        len(dirs) - 1 + (z + 1 < nz).astype(jnp.int32) + (z > 0).astype(jnp.int32),
    )

    def rc(src, dst, ss, rs, dev):
        return pltpu.make_async_remote_copy(
            src_ref=src, dst_ref=dst, send_sem=ss, recv_sem=rs, device_id=dev, device_id_type=MESH
        )

    sent = []

    def begin(src, dst, ss, rs, dev, cond):
        guard(cond, lambda: rc(src, dst, ss, rs, dev).start())
        sent.append((src, dst, ss, rs, dev, cond))

    def both(a, b):
        if a is None:
            return b
        return a if b is None else jnp.logical_and(a, b)

    def pieces(kind, b, t):
        if kind == "land":
            return [(o_buf.at[b, t], r_off.at[b, t], s_off), (l_buf.at[b, t], r_land.at[b, t], s_land)]
        return [(p_buf.at[kind, b, t], r_proj.at[kind, b, t], s_proj.at[kind])]

    def own_src(kind):
        mine = pl.ds(half * hr, hr)
        if kind == "land":
            return [off.at[half], land.at[mine, :]]
        return [proj.at[mine, pl.ds(kind * kc, kc)]]

    def send(kind, b, d, cond=None, own=False):
        dev, exists = peers[d]
        for i, (ref, rs, ss) in enumerate(pieces(kind, b, s)):
            src = own_src(kind)[i] if own else ref
            begin(src, ref, ss.at[d, b], rs, dev, both(cond, exists))

    def await_piece(kind, b, t, cond=None):
        def go():
            for ref, rs, ss in pieces(kind, b, t):
                rc(ref, ref, rs, rs, sib).wait_recv()
        guard(cond, go)

    def send_own(kind):
        for d in dirs:
            send(kind, me, d, own=True)

    def across_of(b):
        return b + 1 - 2 * lax.rem(b, 2)

    def relay(kind, k):
        if k == 0:
            cands = [(me, None, None)]
        else:
            cands = [(me - ny * k, z - k >= 0, UP), (me + ny * k, z + k < nz, DOWN)]
        for b, cond, d in cands:
            if d is not None:
                b = jnp.where(cond, b, me)
                await_piece(kind, b, s, cond)
                send(kind, b, d, cond)
                if ny == 2:
                    send(kind, b, ACROSS, cond)
                send(kind, b, SIB, cond)
        if ny == 2:
            for b, cond, d in cands:
                if d is not None:
                    b = jnp.where(cond, b, me)
                await_piece(kind, across_of(b), s, cond)
                send(kind, across_of(b), SIB, cond)

    my_rows = tiles.at[pl.ds(s * rows_t, rows_t), :]
    begin(my_rows, t_buf.at[pl.ds(rows_t, rows_t), :], t_send, t_recv, mate, None)
    send_own("land")
    own_tiles = pltpu.make_async_copy(my_rows, t_buf.at[pl.ds(0, rows_t), :], loc_sem.at[0])
    own_tiles.start()
    own_off = pltpu.make_async_copy(off.at[half], o_buf.at[me, s], loc_sem.at[1])
    own_off.start()
    own_land = pltpu.make_async_copy(own_src("land")[1], l_buf.at[me, s], loc_sem.at[2])
    own_land.start()
    own_proj = []
    for c in range(chunks):
        cp = pltpu.make_async_copy(own_src(c)[0], p_buf.at[c, me, s], loc_sem.at[3 + c])
        cp.start()
        own_proj.append(cp)

    for k in range(nz):
        relay("land", k)
    for c in range(chunks):
        send_own(c)

    own_tiles.wait()
    own_off.wait()
    own_land.wait()

    def others(kind):
        def body(b, carry):
            await_piece(kind, b, 1 - s)
            return carry
        lax.fori_loop(0, nb, body, 0)

    others("land")
    group = 2 if nb % 2 == 0 else 1
    gw = group * 2 * hr

    def scores(row0):
        def body(i, carry):
            rhs = l_buf[pl.ds(i * group, group)].reshape(gw, l_buf.shape[3])
            sc = lax.dot_general(
                t_buf[pl.ds(row0, rows_t), :], rhs, (((1,), (1,)), ((), ())),
                preferred_element_type=jnp.float32,
            )
            ob = o_buf[pl.ds(i * group, group)]
            ob = (ob[:, 0] + ob[:, 1])
            ob = jnp.concatenate([ob[j] for j in range(group)], axis=1)
            k_buf[i, pl.ds(row0, rows_t), :] = jnp.exp(sc * scale - ob).astype(jnp.bfloat16)
            return carry
        lax.fori_loop(0, nb // group, body, 0)

    scores(0)
    rc(my_rows, t_buf.at[pl.ds(rows_t, rows_t), :], t_send, t_recv, mate).wait_recv()
    scores(rows_t)

    def project(c, row0):
        total = jnp.zeros((rows_t, kc), jnp.float32)
        def body(i, total):
            rhs = p_buf[c, pl.ds(i * group, group)].reshape(gw, kc)
            return total + jnp.dot(
                k_buf[i, pl.ds(row0, rows_t), :], rhs, preferred_element_type=jnp.float32
            )
        return lax.fori_loop(0, nb // group, body, total, unroll=nb <= 8)

    def finish(c):
        rc(x_in.at[c], x_in.at[c], xs_sem.at[c], xr_sem.at[c], mate).wait_recv()
        cols = pl.ds(c * kc, kc)
        full = acc[:, cols] + x_in[c].astype(jnp.float32)
        c_buf[c] = full.astype(jnp.bfloat16)
        where = out.at[pl.ds(s * rows_t, rows_t), cols]
        begin(c_buf.at[c], where, c_send.at[c], c_recv.at[c], sib, None)
        pltpu.make_async_copy(c_buf.at[c], where, c_loc.at[c]).start()
        squares = full * full
        part = squares[:, 0:128]
        for j in range(1, kc // 128):
            part = part + squares[:, j * 128:(j + 1) * 128]
        sq[...] = part if c == 0 else sq[...] + part

    for c in range(chunks):
        for k in range(nz):
            relay(c, k)
        own_proj[c].wait()
        others(c)
        x_out[c] = project(c, rows_t).astype(jnp.bfloat16)
        begin(x_out.at[c], x_in.at[c], xs_sem.at[c], xr_sem.at[c], mate, None)
        acc[:, pl.ds(c * kc, kc)] = project(c, 0)
        if c > 0:
            finish(c - 1)
    finish(chunks - 1)

    total = jnp.sum(sq[...].T, axis=0, keepdims=True)
    e_buf[...] = jnp.log(total / width_k + 1e-6)
    begin(e_buf, energy.at[s], e_sem.at[0], e_sem.at[1], sib, None)
    e_loc = pltpu.make_async_copy(e_buf, energy.at[s], e_sem.at[2])
    e_loc.start()
    e_loc.wait()
    for c in range(chunks):
        cols = pl.ds(c * kc, kc)
        mine = out.at[pl.ds(s * rows_t, rows_t), cols]
        pltpu.make_async_copy(c_buf.at[c], mine, c_loc.at[c]).wait()
        theirs = out.at[pl.ds((1 - s) * rows_t, rows_t), cols]
        rc(c_buf.at[c], theirs, c_send.at[c], c_recv.at[c], sib).wait_recv()
    rc(e_buf, energy.at[1 - s], e_sem.at[0], e_sem.at[1], sib).wait_recv()
    for src, dst, ss, rs, dev, cond in sent:
        guard(cond, lambda: rc(src, dst, ss, rs, dev).wait_send())


def solution(mesh):
    nb = mesh.shape["blk"]
    ny = 2 if nb % 2 == 0 and nb <= 8 else 1

    def per_device(tiles, landmarks, projection, offsets):
        rows, width = tiles.shape
        hr, rows_t = landmarks.shape[0] // 2, rows // 2
        width_k = projection.shape[1]
        chunks = 4
        kc = width_k // chunks
        s = lax.axis_index("split")
        at = lax.broadcasted_iota(jnp.int32, (2, 2, hr), 1) == s
        off = jnp.where(at, offsets.reshape(2, 1, hr), 0.0).reshape(2, 1, 2 * hr)
        group = 2 if nb % 2 == 0 else 1
        bf, f32 = jnp.bfloat16, jnp.float32
        dma = pltpu.SemaphoreType.DMA
        coords, energy = pl.pallas_call(
            functools.partial(kernel, nb, ny, chunks),
            out_shape=(
                jax.ShapeDtypeStruct((rows, width_k), bf),
                jax.ShapeDtypeStruct((2, 1, rows_t), f32),
            ),
            in_specs=[pl.BlockSpec(memory_space=pl.ANY)] * 4,
            out_specs=[pl.BlockSpec(memory_space=pl.ANY)] * 2,
            scratch_shapes=[
                pltpu.VMEM((rows, width), bf),
                pltpu.VMEM((nb, 2, hr, width), bf),
                pltpu.VMEM((nb, 2, 1, 2 * hr), f32),
                pltpu.VMEM((chunks, nb, 2, hr, kc), bf),
                pltpu.VMEM((nb // group, rows, group * 2 * hr), bf),
                pltpu.VMEM((rows_t, width_k), f32),
                pltpu.VMEM((chunks, rows_t, kc), bf),
                pltpu.VMEM((chunks, rows_t, kc), bf),
                pltpu.VMEM((chunks, rows_t, kc), bf),
                pltpu.VMEM((1, rows_t), f32),
                pltpu.VMEM((rows_t, 128), f32),
                dma((nb, 2)), dma((nb, 2)), dma((chunks, nb, 2)),
                dma((4, nb)), dma((4, nb)), dma((chunks, 4, nb)),
                dma((3 + chunks,)), dma, dma, dma((chunks,)), dma((chunks,)),
                dma((chunks,)), dma((chunks,)), dma((chunks,)), dma((3,)),
            ],
            compiler_params=pltpu.CompilerParams(
                collective_id=0, has_side_effects=True, vmem_limit_bytes=56 * 2**20
            ),
        )(tiles, landmarks, projection, off)
        return coords, energy.reshape(rows)

    return jax.shard_map(
        per_device,
        mesh=mesh,
        in_specs=(
            P(("groups", "blk"), None),
            P(("blk", "split"), None),
            P(("blk", "split"), None),
            P(("blk", "split")),
        ),
        out_specs=(P(("groups", "blk"), None), P(("groups", "blk"))),
        check_vma=False,
    )
```

time: 158 us -> 88.2 us (0.56)
  waiting for transfers between devices: 108 us -> 0 us
  Pallas kernels: 0 us -> 82.9 us
  blocking collectives: 24.6 us -> 0 us
  between operations: 13.8 us -> 0.66 us
  matrix products: 6.51 us -> 0 us
  other arithmetic: 2.47 us -> 0.57 us
    all_gather x3 -> x0, waiting for transfers between devices: 99.2 us -> none  [the longest x1 61.2 us: per_device(): lax.all_gather(landmarks, 'blk', axis=0, tiled=True)]
    pallas_call x0 -> x1, Pallas kernels: none -> 82.9 us  [per_device(): pl.pallas_call(functools.partial(kernel, nb, ny, chunks), out_shape=(jax....]
    all_gather x1 -> x0, blocking collectives: 22.2 us -> none  [per_device(): lax.all_gather(offsets.astype(jnp.bfloat16), 'blk', axis=0, tiled=True)]
    reduce_scatter x1 -> x0, waiting for transfers between devices: 7.27 us -> none  [per_device(): lax.psum_scatter(partial_sum.astype(jnp.bfloat16), 'split', scatter_dimen...]
    dot_general x1 -> x0, matrix products: 6.51 us -> none  [block_term(): return jnp.dot(kernel, proj, preferred_element_type=jnp.float32)]
    psum x1 -> x0, blocking collectives: 2.47 us -> none  [per_device(): squares = lax.psum(jnp.sum(share * share, axis=1), 'split')]
  transfers between devices with their start and end apart: 4 -> 0, of which waited for: 4 -> 0; matrix products, arithmetic and copies ran while one was open for 2% -> 0% of each run, Pallas kernels for 0% -> 0%
where the time goes in v1:
time: 88.2 us; the launch traced here: 88 us
  Pallas kernels  82.9 us (94%)
  local copies, waits for them, and re-layouts  3.83 us (4%)
    pallas_call x1, Pallas kernels, per_device(): pl.pallas_call(functools.partial(kernel, nb, ny, chunks), out_shape=(jax....  82.9 us
    unnamed x4, local copies, waits for them, and re-layouts  2.85 us

profile of v1, /device:TPU:0, one launch (start us, length us, event | category | flops | bytes accessed | tf_op | source)
XLA Modules:
  0.0 88.0 jit_solution(17876118728882615457)
XLA Ops:
  0.6 0.1 iota.11
  0.7 0.1 iota.12
  0.8 0.7 broadcast_in_dim.16
  1.5 0.1 broadcast_in_dim.18
  1.6 0.6 broadcast_select_fusion.off
  2.2 82.9 %shard_map.59 = (bf16[512,1024]{1,0:T(8,128)(2,1)}, f32[2,1,256]{2,1,0:T(1,128)}) custom-call(bf16[512,1536]{1,0:T(8,128)(2,1)} %tiles.1, bf16[128,1536]{1,0:T(8,128)(2,1)} %land.1, bf16[128,1024]{1,0:T(8,128)(2,1)} %proj.1, f32[2,1,128]{2,1,0:T(1,128)} %broadcast_select_fusion.off), custom_call_target="tpu_custom_call" | custom-call | tf_op jit(solution)/shard_map/pallas_call | solution.py:246
  85.2 0.0 copy-start
  85.2 2.3 %copy.8 = bf16[512,1024]{1,0:T(8,128)(2,1)} copy(bf16[512,1024]{1,0:T(8,128)(2,1)} %get-tuple-element.8) | data formatting | bytes 2097152
  87.4 0.0 copy-done
  87.4 0.6 copy.9
  (2 shorter events, 0.0 us)
Async XLA Ops:
  85.2 2.3 %copy-start = (f32[2,1,256]{2,1,0:T(1,128)S(1)}, f32[2,1,256]{2,1,0:T(1,128)}, u32[]{:S(2)}) copy-start(f32[2,1,256]{2,1,0:T(1,128)} %get-tuple-element.5) | copy-start | bytes 6148

commit v2 on v1

--- a/solution.py
+++ b/solution.py
@@ -26,6 +26,10 @@
     hr = l_buf.shape[2]
     width_k = acc.shape[1]
     kc = width_k // chunks
+    lp = r_land.shape[0]
+    pr = hr // lp
+    J = lp + chunks
+    lead = 2
     scale = 1.0 / l_buf.shape[3] ** 0.5
 
     mate = {"groups": g + 1 - 2 * half}
@@ -73,16 +77,22 @@
             return b
         return a if b is None else jnp.logical_and(a, b)
 
-    def pieces(kind, b, t):
-        if kind == "land":
-            return [(o_buf.at[b, t], r_off.at[b, t], s_off), (l_buf.at[b, t], r_land.at[b, t], s_land)]
-        return [(p_buf.at[kind, b, t], r_proj.at[kind, b, t], s_proj.at[kind])]
-
-    def own_src(kind):
-        mine = pl.ds(half * hr, hr)
-        if kind == "land":
-            return [off.at[half], land.at[mine, :]]
-        return [proj.at[mine, pl.ds(kind * kc, kc)]]
+    def pieces(j, b, t):
+        if j >= lp:
+            c = j - lp
+            return [(p_buf.at[c, b, t], r_proj.at[c, b, t], s_proj.at[c])]
+        out = [(l_buf.at[b, t, pl.ds(j * pr, pr), :], r_land.at[j, b, t], s_land.at[j])]
+        if j == 0:
+            out.append((o_buf.at[b, t], r_off.at[b, t], s_off))
+        return out
+
+    def own_src(j):
+        if j >= lp:
+            return [proj.at[pl.ds(half * hr, hr), pl.ds((j - lp) * kc, kc)]]
+        out = [land.at[pl.ds(half * hr + j * pr, pr), :]]
+        if j == 0:
+            out.append(off.at[half])
+        return out
 
     def send(kind, b, d, cond=None, own=False):
         dev, exists = peers[d]
@@ -103,45 +113,56 @@
     def across_of(b):
         return b + 1 - 2 * lax.rem(b, 2)
 
-    def relay(kind, k):
-        if k == 0:
-            cands = [(me, None, None)]
-        else:
-            cands = [(me - ny * k, z - k >= 0, UP), (me + ny * k, z + k < nz, DOWN)]
-        for b, cond, d in cands:
+    def cands(k):
+        return [(me - ny * k, z - k >= 0, UP), (me + ny * k, z + k < nz, DOWN)]
+
+    def relay(j, k):
+        for b, cond, d in cands(k):
+            b = jnp.where(cond, b, me)
+            await_piece(j, b, s, cond)
+            send(j, b, d, cond)
+            if ny == 2:
+                send(j, b, ACROSS, cond)
+            send(j, b, SIB, cond)
+
+    def arrive_across(j, k):
+        for b, cond, d in ([(me, None, None)] if k == 0 else cands(k)):
             if d is not None:
                 b = jnp.where(cond, b, me)
-                await_piece(kind, b, s, cond)
-                send(kind, b, d, cond)
-                if ny == 2:
-                    send(kind, b, ACROSS, cond)
-                send(kind, b, SIB, cond)
+            await_piece(j, across_of(b), s, cond)
+            send(j, across_of(b), SIB, cond)
+
+    def step(t):
+        if t < J and t >= lead:
+            send_own(t)
+        for k in range(1, nz):
+            if 0 <= t - k < J:
+                relay(t - k, k)
         if ny == 2:
-            for b, cond, d in cands:
-                if d is not None:
-                    b = jnp.where(cond, b, me)
-                await_piece(kind, across_of(b), s, cond)
-                send(kind, across_of(b), SIB, cond)
+            for k in range(nz):
+                if 0 <= t - 1 - k < J:
+                    arrive_across(t - 1 - k, k)
 
     my_rows = tiles.at[pl.ds(s * rows_t, rows_t), :]
     begin(my_rows, t_buf.at[pl.ds(rows_t, rows_t), :], t_send, t_recv, mate, None)
-    send_own("land")
+    for j in range(lead):
+        send_own(j)
     own_tiles = pltpu.make_async_copy(my_rows, t_buf.at[pl.ds(0, rows_t), :], loc_sem.at[0])
     own_tiles.start()
     own_off = pltpu.make_async_copy(off.at[half], o_buf.at[me, s], loc_sem.at[1])
     own_off.start()
-    own_land = pltpu.make_async_copy(own_src("land")[1], l_buf.at[me, s], loc_sem.at[2])
+    own_land = pltpu.make_async_copy(land.at[pl.ds(half * hr, hr), :], l_buf.at[me, s], loc_sem.at[2])
     own_land.start()
     own_proj = []
     for c in range(chunks):
-        cp = pltpu.make_async_copy(own_src(c)[0], p_buf.at[c, me, s], loc_sem.at[3 + c])
+        cp = pltpu.make_async_copy(own_src(lp + c)[0], p_buf.at[c, me, s], loc_sem.at[3 + c])
         cp.start()
         own_proj.append(cp)
 
-    for k in range(nz):
-        relay("land", k)
-    for c in range(chunks):
-        send_own(c)
+    last = nz - 1 + (1 if ny == 2 else 0)
+    for t in range(lp + last):
+        step(t)
+    step(lp + last)
 
     own_tiles.wait()
     own_off.wait()
@@ -153,7 +174,8 @@
             return carry
         lax.fori_loop(0, nb, body, 0)
 
-    others("land")
+    for j in range(lp):
+        others(j)
     group = 2 if nb % 2 == 0 else 1
     gw = group * 2 * hr
 
@@ -165,8 +187,7 @@
                 preferred_element_type=jnp.float32,
             )
             ob = o_buf[pl.ds(i * group, group)]
-            ob = (ob[:, 0] + ob[:, 1])
-            ob = jnp.concatenate([ob[j] for j in range(group)], axis=1)
+            ob = jnp.concatenate([ob[j, t] for j in range(group) for t in range(2)], axis=1)
             k_buf[i, pl.ds(row0, rows_t), :] = jnp.exp(sc * scale - ob).astype(jnp.bfloat16)
             return carry
         lax.fori_loop(0, nb // group, body, 0)
@@ -199,10 +220,9 @@
         sq[...] = part if c == 0 else sq[...] + part
 
     for c in range(chunks):
-        for k in range(nz):
-            relay(c, k)
+        step(lp + last + c + 1)
         own_proj[c].wait()
-        others(c)
+        others(lp + c)
         x_out[c] = project(c, rows_t).astype(jnp.bfloat16)
         begin(x_out.at[c], x_in.at[c], xs_sem.at[c], xr_sem.at[c], mate, None)
         acc[:, pl.ds(c * kc, kc)] = project(c, 0)
@@ -237,9 +257,8 @@
         width_k = projection.shape[1]
         chunks = 4
         kc = width_k // chunks
-        s = lax.axis_index("split")
-        at = lax.broadcasted_iota(jnp.int32, (2, 2, hr), 1) == s
-        off = jnp.where(at, offsets.reshape(2, 1, hr), 0.0).reshape(2, 1, 2 * hr)
+        lp = 4 if hr % 64 == 0 and nb <= 8 else 1
+        off = offsets.reshape(2, 1, hr)
         group = 2 if nb % 2 == 0 else 1
         bf, f32 = jnp.bfloat16, jnp.float32
         dma = pltpu.SemaphoreType.DMA
@@ -254,7 +273,7 @@
             scratch_shapes=[
                 pltpu.VMEM((rows, width), bf),
                 pltpu.VMEM((nb, 2, hr, width), bf),
-                pltpu.VMEM((nb, 2, 1, 2 * hr), f32),
+                pltpu.VMEM((nb, 2, 1, hr), f32),
                 pltpu.VMEM((chunks, nb, 2, hr, kc), bf),
                 pltpu.VMEM((nb // group, rows, group * 2 * hr), bf),
                 pltpu.VMEM((rows_t, width_k), f32),
@@ -263,8 +282,8 @@
                 pltpu.VMEM((chunks, rows_t, kc), bf),
                 pltpu.VMEM((1, rows_t), f32),
                 pltpu.VMEM((rows_t, 128), f32),
-                dma((nb, 2)), dma((nb, 2)), dma((chunks, nb, 2)),
-                dma((4, nb)), dma((4, nb)), dma((chunks, 4, nb)),
+                dma((lp, nb, 2)), dma((nb, 2)), dma((chunks, nb, 2)),
+                dma((lp, 4, nb)), dma((4, nb)), dma((chunks, 4, nb)),
                 dma((3 + chunks,)), dma, dma, dma((chunks,)), dma((chunks,)),
                 dma((chunks,)), dma((chunks,)), dma((chunks,)), dma((3,)),
             ],

time: 88.2 us -> 60.1 us (0.68)
  Pallas kernels: 82.9 us -> 54.9 us
    pallas_call x1, Pallas kernels: 82.9 us -> 54.9 us  [per_device(): pl.pallas_call(functools.partial(kernel, nb, ny, chunks), out_shape=(jax....]
    reshape x0 -> x1, local copies, waits for them, and re-layouts: none -> 1.3 us  [per_device(): off = offsets.reshape(2, 1, hr)]
where the time goes in v2:
time: 60.1 us; the launch traced here: 59.7 us
  Pallas kernels  54.9 us (91%)
  local copies, waits for them, and re-layouts  4.14 us (7%)
  between operations  0.65 us (1%)
    pallas_call x1, Pallas kernels, per_device(): pl.pallas_call(functools.partial(kernel, nb, ny, chunks), out_shape=(jax....  54.9 us
    unnamed x4, local copies, waits for them, and re-layouts  2.85 us
    reshape x1, local copies, waits for them, and re-layouts, per_device(): off = offsets.reshape(2, 1, hr)  1.3 us

profile of v2, /device:TPU:0, one launch (start us, length us, event | category | flops | bytes accessed | tf_op | source)
XLA Modules:
  0.0 59.7 jit_solution(1652061047106184892)
XLA Ops:
  0.6 1.3 %reshape.10 = f32[2,1,64]{2,0,1:T(2,128)} reshape(f32[128]{0:T(128)} %param.7) | data formatting | bytes 1024 | tf_op jit(solution)/shard_map/reshape | solution.py:261
  1.9 54.9 %shard_map.59 = (bf16[512,1024]{1,0:T(8,128)(2,1)}, f32[2,1,256]{2,1,0:T(1,128)}) custom-call(bf16[512,1536]{1,0:T(8,128)(2,1)} %tiles.1, bf16[128,1536]{1,0:T(8,128)(2,1)} %land.1, bf16[128,1024]{1,0:T(8,128)(2,1)} %proj.1, f32[2,1,64]{2,1,0:T(1,128)} %bitcast.3), custom_call_target="tpu_custom_call" | custom-call | tf_op jit(solution)/shard_map/pallas_call | solution.py:265
  56.9 0.0 copy-start
  56.9 2.3 %copy.9 = bf16[512,1024]{1,0:T(8,128)(2,1)} copy(bf16[512,1024]{1,0:T(8,128)(2,1)} %get-tuple-element.8) | data formatting | bytes 2097152
  59.1 0.0 copy-done
  59.1 0.6 copy.10
Async XLA Ops:
  56.9 2.3 %copy-start = (f32[2,1,256]{2,1,0:T(1,128)S(1)}, f32[2,1,256]{2,1,0:T(1,128)}, u32[]{:S(2)}) copy-start(f32[2,1,256]{2,1,0:T(1,128)} %get-tuple-element.5) | copy-start | bytes 6148

commit v3 on v2

--- a/solution.py
+++ b/solution.py
@@ -30,6 +30,7 @@
     pr = hr // lp
     J = lp + chunks
     lead = 2
+    turned = (lp, lp + 2) if ny == 2 else ()
     scale = 1.0 / l_buf.shape[3] ** 0.5
 
     mate = {"groups": g + 1 - 2 * half}
@@ -121,7 +122,7 @@
             b = jnp.where(cond, b, me)
             await_piece(j, b, s, cond)
             send(j, b, d, cond)
-            if ny == 2:
+            if ny == 2 and j not in turned:
                 send(j, b, ACROSS, cond)
             send(j, b, SIB, cond)
 
@@ -129,15 +130,21 @@
         for b, cond, d in ([(me, None, None)] if k == 0 else cands(k)):
             if d is not None:
                 b = jnp.where(cond, b, me)
-            await_piece(j, across_of(b), s, cond)
-            send(j, across_of(b), SIB, cond)
-
-    def step(t):
+            b = across_of(b)
+            await_piece(j, b, s, cond)
+            if j in turned:
+                for way in ([UP, DOWN] if d is None else [d]):
+                    send(j, b, way, cond)
+            send(j, b, SIB, cond)
+
+    def relays(t):
         if t < J and t >= lead:
             send_own(t)
         for k in range(1, nz):
             if 0 <= t - k < J:
                 relay(t - k, k)
+
+    def crossings(t):
         if ny == 2:
             for k in range(nz):
                 if 0 <= t - 1 - k < J:
@@ -161,8 +168,9 @@
 
     last = nz - 1 + (1 if ny == 2 else 0)
     for t in range(lp + last):
-        step(t)
-    step(lp + last)
+        relays(t)
+        crossings(t)
+    relays(lp + last)
 
     own_tiles.wait()
     own_off.wait()
@@ -220,7 +228,8 @@
         sq[...] = part if c == 0 else sq[...] + part
 
     for c in range(chunks):
-        step(lp + last + c + 1)
+        crossings(lp + last + c)
+        relays(lp + last + c + 1)
         own_proj[c].wait()
         others(lp + c)
         x_out[c] = project(c, rows_t).astype(jnp.bfloat16)
@@ -247,6 +256,21 @@
         guard(cond, lambda: rc(src, dst, ss, rs, dev).wait_send())
 
 
+def write_out(coords, energy, coords_out, energy_out, sem):
+    n = sem.shape[0]
+    rows = coords.shape[0] // n
+    half = energy.shape[2]
+    copies = []
+    for i in range(n):
+        part = pl.ds(i * rows, rows)
+        copies.append(pltpu.make_async_copy(coords.at[part, :], coords_out.at[part, :], sem.at[i]))
+        copies[-1].start()
+    for i in range(2):
+        energy_out[pl.ds(i * half, half)] = energy[i, 0, :]
+    for copy in copies:
+        copy.wait()
+
+
 def solution(mesh):
     nb = mesh.shape["blk"]
     ny = 2 if nb % 2 == 0 and nb <= 8 else 1
@@ -257,7 +281,7 @@
         width_k = projection.shape[1]
         chunks = 4
         kc = width_k // chunks
-        lp = 4 if hr % 64 == 0 and nb <= 8 else 1
+        lp = 2 if hr % 32 == 0 and nb <= 8 else 1
         off = offsets.reshape(2, 1, hr)
         group = 2 if nb % 2 == 0 else 1
         bf, f32 = jnp.bfloat16, jnp.float32
@@ -291,7 +315,16 @@
                 collective_id=0, has_side_effects=True, vmem_limit_bytes=56 * 2**20
             ),
         )(tiles, landmarks, projection, off)
-        return coords, energy.reshape(rows)
+        return pl.pallas_call(
+            write_out,
+            out_shape=(
+                jax.ShapeDtypeStruct((rows, width_k), bf),
+                jax.ShapeDtypeStruct((rows,), f32),
+            ),
+            in_specs=[pl.BlockSpec(memory_space=pl.ANY), pl.BlockSpec(memory_space=pltpu.VMEM)],
+            out_specs=(pl.BlockSpec(memory_space=pl.ANY), pl.BlockSpec(memory_space=pltpu.VMEM)),
+            scratch_shapes=[dma((8,))],
+        )(coords, energy)
 
     return jax.shard_map(
         per_device,

time: 60.1 us -> 89.9 us (1.50)
  Pallas kernels: 54.9 us -> 87.6 us
  local copies, waits for them, and re-layouts: 4.14 us -> 1.3 us
    pallas_call x0 -> x1, Pallas kernels: none -> 34.2 us  [per_device(): pl.pallas_call(write_out, out_shape=(jax.ShapeDtypeStruct((rows, width_k)...]
    unnamed x4 -> x0, local copies, waits for them, and re-layouts: 2.85 us -> none
    pallas_call x1, Pallas kernels: 54.9 us -> 53.4 us  [per_device(): pl.pallas_call(functools.partial(kernel, nb, ny, chunks), out_shape=(jax....]
where the time goes in v3:
time: 89.9 us; the launch traced here: 89.5 us
  Pallas kernels  87.6 us (97%)
  local copies, waits for them, and re-layouts  1.3 us (1%)
    pallas_call x1, Pallas kernels, per_device(): pl.pallas_call(functools.partial(kernel, nb, ny, chunks), out_shape=(jax....  53.4 us
    pallas_call x1, Pallas kernels, per_device(): pl.pallas_call(write_out, out_shape=(jax.ShapeDtypeStruct((rows, width_k)...  34.2 us

profile of v3, /device:TPU:0, one launch (start us, length us, event | category | flops | bytes accessed | tf_op | source)
XLA Modules:
  0.0 89.5 jit_solution(2927933829598513290)
XLA Ops:
  0.6 1.3 %reshape.7 = f32[2,1,64]{2,0,1:T(2,128)} reshape(f32[128]{0:T(128)} %param.7) | data formatting | bytes 1024 | tf_op jit(solution)/shard_map/reshape | solution.py:285
  1.9 53.4 %shard_map.59 = (bf16[512,1024]{1,0:T(8,128)(2,1)}, f32[2,1,256]{2,1,0:T(1,128)}) custom-call(bf16[512,1536]{1,0:T(8,128)(2,1)} %tiles.1, bf16[128,1536]{1,0:T(8,128)(2,1)} %land.1, bf16[128,1024]{1,0:T(8,128)(2,1)} %proj.1, f32[2,1,64]{2,1,0:T(1,128)} %bitcast.1), custom_call_target="tpu_custom_call" | custom-call | tf_op jit(solution)/shard_map/pallas_call | solution.py:289
  55.3 34.2 %shard_map.60 = (bf16[512,1024]{1,0:T(8,128)(2,1)}, f32[512]{0:T(512)}) custom-call(bf16[512,1024]{1,0:T(8,128)(2,1)} %get-tuple-element.4.coords, f32[2,1,256]{2,1,0:T(1,128)} %get-tuple-element.5.energy), custom_call_target="tpu_custom_call" | custom-call | tf_op jit(solution)/shard_map/pallas_call | solution.py:318

commit v4 on v2

--- a/solution.py
+++ b/solution.py
@@ -30,6 +30,7 @@
     pr = hr // lp
     J = lp + chunks
     lead = 2
+    turned = (lp,) if ny == 2 else ()
     scale = 1.0 / l_buf.shape[3] ** 0.5
 
     mate = {"groups": g + 1 - 2 * half}
@@ -91,7 +92,7 @@
             return [proj.at[pl.ds(half * hr, hr), pl.ds((j - lp) * kc, kc)]]
         out = [land.at[pl.ds(half * hr + j * pr, pr), :]]
         if j == 0:
-            out.append(off.at[half])
+            out.append(off)
         return out
 
     def send(kind, b, d, cond=None, own=False):
@@ -121,7 +122,7 @@
             b = jnp.where(cond, b, me)
             await_piece(j, b, s, cond)
             send(j, b, d, cond)
-            if ny == 2:
+            if ny == 2 and j not in turned:
                 send(j, b, ACROSS, cond)
             send(j, b, SIB, cond)
 
@@ -129,27 +130,33 @@
         for b, cond, d in ([(me, None, None)] if k == 0 else cands(k)):
             if d is not None:
                 b = jnp.where(cond, b, me)
-            await_piece(j, across_of(b), s, cond)
-            send(j, across_of(b), SIB, cond)
-
-    def step(t):
+            b = across_of(b)
+            await_piece(j, b, s, cond)
+            if j in turned:
+                for way in ([UP, DOWN] if d is None else [d]):
+                    send(j, b, way, cond)
+            send(j, b, SIB, cond)
+
+    def relays(t):
         if t < J and t >= lead:
             send_own(t)
         for k in range(1, nz):
             if 0 <= t - k < J:
                 relay(t - k, k)
+
+    def crossings(t):
         if ny == 2:
             for k in range(nz):
                 if 0 <= t - 1 - k < J:
                     arrive_across(t - 1 - k, k)
 
     my_rows = tiles.at[pl.ds(s * rows_t, rows_t), :]
-    begin(my_rows, t_buf.at[pl.ds(rows_t, rows_t), :], t_send, t_recv, mate, None)
     for j in range(lead):
         send_own(j)
+    begin(my_rows, t_buf.at[pl.ds(rows_t, rows_t), :], t_send, t_recv, mate, None)
     own_tiles = pltpu.make_async_copy(my_rows, t_buf.at[pl.ds(0, rows_t), :], loc_sem.at[0])
     own_tiles.start()
-    own_off = pltpu.make_async_copy(off.at[half], o_buf.at[me, s], loc_sem.at[1])
+    own_off = pltpu.make_async_copy(off, o_buf.at[me, s], loc_sem.at[1])
     own_off.start()
     own_land = pltpu.make_async_copy(land.at[pl.ds(half * hr, hr), :], l_buf.at[me, s], loc_sem.at[2])
     own_land.start()
@@ -161,8 +168,9 @@
 
     last = nz - 1 + (1 if ny == 2 else 0)
     for t in range(lp + last):
-        step(t)
-    step(lp + last)
+        relays(t)
+        crossings(t)
+    relays(lp + last)
 
     own_tiles.wait()
     own_off.wait()
@@ -187,7 +195,8 @@
                 preferred_element_type=jnp.float32,
             )
             ob = o_buf[pl.ds(i * group, group)]
-            ob = jnp.concatenate([ob[j, t] for j in range(group) for t in range(2)], axis=1)
+            ob = [jnp.where(half == 0, ob[j, t][:, :hr], ob[j, t][:, hr:]) for j in range(group) for t in range(2)]
+            ob = jnp.concatenate(ob, axis=1)
             k_buf[i, pl.ds(row0, rows_t), :] = jnp.exp(sc * scale - ob).astype(jnp.bfloat16)
             return carry
         lax.fori_loop(0, nb // group, body, 0)
@@ -220,7 +229,8 @@
         sq[...] = part if c == 0 else sq[...] + part
 
     for c in range(chunks):
-        step(lp + last + c + 1)
+        crossings(lp + last + c)
+        relays(lp + last + c + 1)
         own_proj[c].wait()
         others(lp + c)
         x_out[c] = project(c, rows_t).astype(jnp.bfloat16)
@@ -255,10 +265,10 @@
         rows, width = tiles.shape
         hr, rows_t = landmarks.shape[0] // 2, rows // 2
         width_k = projection.shape[1]
-        chunks = 4
+        chunks = 2
         kc = width_k // chunks
-        lp = 4 if hr % 64 == 0 and nb <= 8 else 1
-        off = offsets.reshape(2, 1, hr)
+        lp = 2 if hr % 32 == 0 and nb <= 8 else 1
+        off = offsets.reshape(1, 2 * hr)
         group = 2 if nb % 2 == 0 else 1
         bf, f32 = jnp.bfloat16, jnp.float32
         dma = pltpu.SemaphoreType.DMA
@@ -273,7 +283,7 @@
             scratch_shapes=[
                 pltpu.VMEM((rows, width), bf),
                 pltpu.VMEM((nb, 2, hr, width), bf),
-                pltpu.VMEM((nb, 2, 1, hr), f32),
+                pltpu.VMEM((nb, 2, 1, 2 * hr), f32),
                 pltpu.VMEM((chunks, nb, 2, hr, kc), bf),
                 pltpu.VMEM((nb // group, rows, group * 2 * hr), bf),
                 pltpu.VMEM((rows_t, width_k), f32),

time: 60.1 us -> 56.1 us (0.933)
  Pallas kernels: 54.9 us -> 52.4 us
  local copies, waits for them, and re-layouts: 4.14 us -> 2.85 us
    pallas_call x1, Pallas kernels: 54.9 us -> 52.4 us  [per_device(): pl.pallas_call(functools.partial(kernel, nb, ny, chunks), out_shape=(jax....]
    reshape x1 -> x0, local copies, waits for them, and re-layouts: 1.3 us -> none  [per_device(): off = offsets.reshape(2, 1, hr)]
where the time goes in v4:
time: 56.1 us; the launch traced here: 55.9 us
  Pallas kernels  52.4 us (93%)
  local copies, waits for them, and re-layouts  2.85 us (5%)
  between operations  0.65 us (1%)
    pallas_call x1, Pallas kernels, per_device(): pl.pallas_call(functools.partial(kernel, nb, ny, chunks), out_shape=(jax....  52.4 us
    unnamed x4, local copies, waits for them, and re-layouts  2.85 us

profile of v4, /device:TPU:0, one launch (start us, length us, event | category | flops | bytes accessed | tf_op | source)
XLA Modules:
  0.0 55.9 jit_solution(15252420727078897251)
XLA Ops:
  0.6 52.4 %shard_map.59 = (bf16[512,1024]{1,0:T(8,128)(2,1)}, f32[2,1,256]{2,1,0:T(1,128)}) custom-call(bf16[512,1536]{1,0:T(8,128)(2,1)} %tiles.1, bf16[128,1536]{1,0:T(8,128)(2,1)} %land.1, bf16[128,1024]{1,0:T(8,128)(2,1)} %proj.1, f32[1,128]{1,0:T(1,128)} %bitcast.3), custom_call_target="tpu_custom_call" | custom-call | tf_op jit(solution)/shard_map/pallas_call | solution.py:275
  53.1 0.0 copy-start
  53.1 2.3 %copy.8 = bf16[512,1024]{1,0:T(8,128)(2,1)} copy(bf16[512,1024]{1,0:T(8,128)(2,1)} %get-tuple-element.8) | data formatting | bytes 2097152
  55.4 0.0 copy-done
  55.4 0.6 %copy.9 = f32[512]{0:T(512)} copy(f32[512]{0:T(512)S(1)} %bitcast.2) | data formatting | bytes 4096
Async XLA Ops:
  53.1 2.3 %copy-start = (f32[2,1,256]{2,1,0:T(1,128)S(1)}, f32[2,1,256]{2,1,0:T(1,128)}, u32[]{:S(2)}) copy-start(f32[2,1,256]{2,1,0:T(1,128)} %get-tuple-element.5) | copy-start | bytes 6148

commit v5 on v4

--- a/solution.py
+++ b/solution.py
@@ -26,6 +26,8 @@
     hr = l_buf.shape[2]
     width_k = acc.shape[1]
     kc = width_k // chunks
+    kw = x_in.shape[2]
+    sub = kc // kw
     lp = r_land.shape[0]
     pr = hr // lp
     J = lp + chunks
@@ -205,18 +207,18 @@
     rc(my_rows, t_buf.at[pl.ds(rows_t, rows_t), :], t_send, t_recv, mate).wait_recv()
     scores(rows_t)
 
-    def project(c, row0):
-        total = jnp.zeros((rows_t, kc), jnp.float32)
+    def project(c, q, row0):
         def body(i, total):
-            rhs = p_buf[c, pl.ds(i * group, group)].reshape(gw, kc)
+            rhs = p_buf[c, pl.ds(i * group, group), :, :, q * kw:(q + 1) * kw].reshape(gw, kw)
             return total + jnp.dot(
                 k_buf[i, pl.ds(row0, rows_t), :], rhs, preferred_element_type=jnp.float32
             )
+        total = jnp.zeros((rows_t, kw), jnp.float32)
         return lax.fori_loop(0, nb // group, body, total, unroll=nb <= 8)
 
     def finish(c):
         rc(x_in.at[c], x_in.at[c], xs_sem.at[c], xr_sem.at[c], mate).wait_recv()
-        cols = pl.ds(c * kc, kc)
+        cols = pl.ds(c * kw, kw)
         full = acc[:, cols] + x_in[c].astype(jnp.float32)
         c_buf[c] = full.astype(jnp.bfloat16)
         where = out.at[pl.ds(s * rows_t, rows_t), cols]
@@ -224,7 +226,7 @@
         pltpu.make_async_copy(c_buf.at[c], where, c_loc.at[c]).start()
         squares = full * full
         part = squares[:, 0:128]
-        for j in range(1, kc // 128):
+        for j in range(1, kw // 128):
             part = part + squares[:, j * 128:(j + 1) * 128]
         sq[...] = part if c == 0 else sq[...] + part
 
@@ -233,12 +235,17 @@
         relays(lp + last + c + 1)
         own_proj[c].wait()
         others(lp + c)
-        x_out[c] = project(c, rows_t).astype(jnp.bfloat16)
-        begin(x_out.at[c], x_in.at[c], xs_sem.at[c], xr_sem.at[c], mate, None)
-        acc[:, pl.ds(c * kc, kc)] = project(c, 0)
+        for q in range(sub):
+            i = c * sub + q
+            x_out[i] = project(c, q, rows_t).astype(jnp.bfloat16)
+            begin(x_out.at[i], x_in.at[i], xs_sem.at[i], xr_sem.at[i], mate, None)
+        for q in range(sub):
+            acc[:, pl.ds(c * kc + q * kw, kw)] = project(c, q, 0)
         if c > 0:
-            finish(c - 1)
-    finish(chunks - 1)
+            for q in range(sub):
+                finish((c - 1) * sub + q)
+    for q in range(sub):
+        finish((chunks - 1) * sub + q)
 
     total = jnp.sum(sq[...].T, axis=0, keepdims=True)
     e_buf[...] = jnp.log(total / width_k + 1e-6)
@@ -246,8 +253,8 @@
     e_loc = pltpu.make_async_copy(e_buf, energy.at[s], e_sem.at[2])
     e_loc.start()
     e_loc.wait()
-    for c in range(chunks):
-        cols = pl.ds(c * kc, kc)
+    for c in range(chunks * sub):
+        cols = pl.ds(c * kw, kw)
         mine = out.at[pl.ds(s * rows_t, rows_t), cols]
         pltpu.make_async_copy(c_buf.at[c], mine, c_loc.at[c]).wait()
         theirs = out.at[pl.ds((1 - s) * rows_t, rows_t), cols]
@@ -265,7 +272,7 @@
         rows, width = tiles.shape
         hr, rows_t = landmarks.shape[0] // 2, rows // 2
         width_k = projection.shape[1]
-        chunks = 2
+        chunks, sub = 2, 2
         kc = width_k // chunks
         lp = 2 if hr % 32 == 0 and nb <= 8 else 1
         off = offsets.reshape(1, 2 * hr)
@@ -287,15 +294,15 @@
                 pltpu.VMEM((chunks, nb, 2, hr, kc), bf),
                 pltpu.VMEM((nb // group, rows, group * 2 * hr), bf),
                 pltpu.VMEM((rows_t, width_k), f32),
-                pltpu.VMEM((chunks, rows_t, kc), bf),
-                pltpu.VMEM((chunks, rows_t, kc), bf),
-                pltpu.VMEM((chunks, rows_t, kc), bf),
+                pltpu.VMEM((chunks * sub, rows_t, kc // sub), bf),
+                pltpu.VMEM((chunks * sub, rows_t, kc // sub), bf),
+                pltpu.VMEM((chunks * sub, rows_t, kc // sub), bf),
                 pltpu.VMEM((1, rows_t), f32),
                 pltpu.VMEM((rows_t, 128), f32),
                 dma((lp, nb, 2)), dma((nb, 2)), dma((chunks, nb, 2)),
                 dma((lp, 4, nb)), dma((4, nb)), dma((chunks, 4, nb)),
-                dma((3 + chunks,)), dma, dma, dma((chunks,)), dma((chunks,)),
-                dma((chunks,)), dma((chunks,)), dma((chunks,)), dma((3,)),
+                dma((3 + chunks,)), dma, dma, dma((chunks * sub,)), dma((chunks * sub,)),
+                dma((chunks * sub,)), dma((chunks * sub,)), dma((chunks * sub,)), dma((3,)),
             ],
             compiler_params=pltpu.CompilerParams(
                 collective_id=0, has_side_effects=True, vmem_limit_bytes=56 * 2**20

time: 56.1 us -> 55.9 us (level)
  no operation moved by 1% of the time
where the time goes in v5:
time: 55.9 us; the launch traced here: 55.8 us
  Pallas kernels  52.3 us (94%)
  local copies, waits for them, and re-layouts  2.85 us (5%)
  between operations  0.65 us (1%)
    pallas_call x1, Pallas kernels, per_device(): pl.pallas_call(functools.partial(kernel, nb, ny, chunks), out_shape=(jax....  52.3 us
    unnamed x4, local copies, waits for them, and re-layouts  2.85 us

profile of v5, /device:TPU:0, one launch (start us, length us, event | category | flops | bytes accessed | tf_op | source)
XLA Modules:
  0.0 55.8 jit_solution(10367592653002895565)
XLA Ops:
  0.6 52.3 %shard_map.59 = (bf16[512,1024]{1,0:T(8,128)(2,1)}, f32[2,1,256]{2,1,0:T(1,128)}) custom-call(bf16[512,1536]{1,0:T(8,128)(2,1)} %tiles.1, bf16[128,1536]{1,0:T(8,128)(2,1)} %land.1, bf16[128,1024]{1,0:T(8,128)(2,1)} %proj.1, f32[1,128]{1,0:T(1,128)} %bitcast.3), custom_call_target="tpu_custom_call" | custom-call | tf_op jit(solution)/shard_map/pallas_call | solution.py:282
  52.9 0.0 copy-start
  52.9 2.3 %copy.8 = bf16[512,1024]{1,0:T(8,128)(2,1)} copy(bf16[512,1024]{1,0:T(8,128)(2,1)} %get-tuple-element.8) | data formatting | bytes 2097152
  55.2 0.0 copy-done
  55.2 0.6 %copy.9 = f32[512]{0:T(512)} copy(f32[512]{0:T(512)S(1)} %bitcast.2) | data formatting | bytes 4096
Async XLA Ops:
  52.9 2.3 %copy-start = (f32[2,1,256]{2,1,0:T(1,128)S(1)}, f32[2,1,256]{2,1,0:T(1,128)}, u32[]{:S(2)}) copy-start(f32[2,1,256]{2,1,0:T(1,128)} %get-tuple-element.5) | copy-start | bytes 6148
